TPU v7x, 512 devices: a whole 4x8x8 slice. The times are simulated.
512 devices in a mesh: groups: 512 (over x, z, y, core).
Axes of the slice: x: 4, y: 8, z: 8, core: 2. Of those that a mesh axis runs over, the one named last changes fastest.
Arguments:
- currents: bfloat16 [2, 192, 262144], P(None, None, 'groups'), may hold values from -6 to 6
- inverse: bfloat16 [512, 2, 1024, 1024], P('groups'), may hold values from -0.125 to 0.125
- send_blocks: int32 [512, 4], P('groups'), may hold values from 0 to 3
- send_flags: int32 [512, 4], P('groups'), may hold values 0 or 1
Outputs:
- precond: bfloat16 [2, 192, 262144], P(None, None, 'groups')
Inputs may be any that keep to these rules, and one draw needn't show every extreme that they name: `send_blocks`: a block index of the lending group's own rows.
All inputs are finite; a program needn't handle non-finite values. No bound on the sum of `send_flags` on one device may be relied on, other than what follows from the above.
Results may differ from a plain program's by a relative error of at most 0.0037.
Values may be sent and summed in bfloat16 or wider, within the bound.
A program may use at most 64 MiB of HBM per device.

v0:
```python
import jax
import jax.numpy as jnp
from jax import lax
from jax.sharding import PartitionSpec as P

BLK = 128
COLS = 8
OWN = 512


def from_partner(value, axis, distance):
    return lax.ppermute(value, axis, [(i, i ^ 1 << distance) for i in range(lax.axis_size(axis))])


def passed_along(value, axis, steps):
    count = lax.axis_size(axis)
    pairs = [(source, (source + steps) % count) for source in range(count)]
    return lax.ppermute(value, axis, pairs)


def complex_apply(values, matrix):
    prod = jnp.einsum("prk,qjk->prqj", values, matrix, preferred_element_type=jnp.float32)
    return jnp.stack([prod[0, :, 0] - prod[1, :, 1], prod[0, :, 1] + prod[1, :, 0]])


def lend_rounds(payloads):
    incoming = [None, None, None, None]
    line_bit = COLS.bit_length() - 1
    incoming[0] = from_partner(payloads[0], "groups", 0)
    incoming[2] = from_partner(payloads[2], "groups", line_bit)
    for round_no in (1, 3):
        stride = 1 if round_no < 2 else COLS
        bit_no = 0 if round_no < 2 else line_bit
        moved = passed_along(payloads[round_no], "groups", stride)
        moved = from_partner(moved, "groups", bit_no)
        incoming[round_no] = passed_along(moved, "groups", -stride)
    return incoming


def body(currents, inverse, send_blocks, send_flags):
    matrix = inverse[0]
    active = [send_flags[0, round_no] for round_no in range(4)]
    starts = [send_blocks[0, round_no] * BLK for round_no in range(4)]
    outgoing = []
    for round_no in range(4):
        piece = lax.dynamic_slice_in_dim(currents, starts[round_no], BLK, 2)
        outgoing.append(piece * active[round_no].astype(jnp.bfloat16))
    incoming = lend_rounds(outgoing)
    box = jnp.concatenate([currents] + incoming, axis=2)
    local = complex_apply(box, matrix)
    returning = [
        local[:, :, OWN + round_no * BLK : OWN + (round_no + 1) * BLK].astype(jnp.bfloat16)
        for round_no in range(4)
    ]
    arrived = lend_rounds(returning)
    total = local[:, :, :OWN]
    for round_no in range(4):
        segment = lax.dynamic_slice_in_dim(total, starts[round_no], BLK, 2)
        added = segment + arrived[round_no].astype(jnp.float32) * active[round_no].astype(
            jnp.float32
        )
        total = lax.dynamic_update_slice_in_dim(total, added, starts[round_no], 2)
    return total.astype(jnp.bfloat16)


def solution(mesh):
    in_specs = (
        P(None, None, "groups"),
        P("groups", None, None, None),
        P("groups", None),
        P("groups", None),
    )
    out_specs = P(None, None, "groups")
    return jax.shard_map(body, mesh=mesh, in_specs=in_specs, out_specs=out_specs, check_vma=False)
```

profile of v0, /device:TPU:16, one launch (start us, length us, event | category | flops | bytes accessed | tf_op | source)
XLA Modules:
  0.0 111.0 jit_solution(17639489700446147082)
XLA Ops:
  3.9 1.5 %fusion.8 = (s32[1,1]{1,0:T(1,128)}, s32[1,1]{1,0:T(1,128)}, s32[1,1]{1,0:T(1,128)}, s32[1,1]{1,0:T(1,128)}) fusion(s32[1,4]{1,0:T(1,128)} %param.7), kind=kLoop, calls=%fused_computation.26 | loop fusion | bytes 32 | tf_op jit(solution)/shard_map/slice | solution.py:42
  9.0 1.9 %collective-permute-start.1 = (bf16[2,192,128]{2,1,0:T(8,128)(2,1)S(1)}, bf16[2,192,128]{2,1,0:T(8,128)(2,1)S(1)}, u32[]{:S(2)}, u32[]{:S(2)}) collective-permute-start(bf16[2,192,128]{2,1,0:T(8,128)(2,1)S(1)} %get-tuple-element.13), channel_id=1, source_target_pairs={{0,1},{1,2},{2,3},{3,4},{4,5},{5,6},{6,7},{7,8},{8,9},{9,10},{10,1... | collective-permute-start | bytes 294920 | tf_op jit(solution)/shard_map/ppermute | solution.py:18
  10.9 5.9 %collective-permute-start.5 = (bf16[2,192,128]{2,1,0:T(8,128)(2,1)S(1)}, bf16[2,192,128]{2,1,0:T(8,128)(2,1)S(1)}, u32[]{:S(2)}, u32[]{:S(2)}) collective-permute-start(bf16[2,192,128]{2,1,0:T(8,128)(2,1)S(1)} %get-tuple-element.11), channel_id=1, source_target_pairs={{0,8},{1,9},{2,10},{3,11},{4,12},{5,13},{6,14},{7,15},{8,16},{9,17... | collective-permute-start | bytes 294920 | tf_op jit(solution)/shard_map/ppermute | solution.py:18
  16.9 5.6 %collective-permute-start.4 = (bf16[2,192,128]{2,1,0:T(8,128)(2,1)S(1)}, bf16[2,192,128]{2,1,0:T(8,128)(2,1)S(1)}, u32[]{:S(2)}, u32[]{:S(2)}) collective-permute-start(bf16[2,192,128]{2,1,0:T(8,128)(2,1)S(1)} %get-tuple-element.12), channel_id=1, source_target_pairs={{0,8},{1,9},{2,10},{3,11},{4,12},{5,13},{6,14},{7,15},{8,0},{9,1},... | collective-permute-start | bytes 294920 | tf_op jit(solution)/shard_map/ppermute | solution.py:12
  22.5 3.0 %collective-permute-start = (bf16[2,192,128]{2,1,0:T(8,128)(2,1)S(1)}, bf16[2,192,128]{2,1,0:T(8,128)(2,1)S(1)}, u32[]{:S(2)}, u32[]{:S(2)}) collective-permute-start(bf16[2,192,128]{2,1,0:T(8,128)(2,1)S(1)} %get-tuple-element.14), channel_id=1, source_target_pairs={{0,1},{1,0},{2,3},{3,2},{4,5},{5,4},{6,7},{7,6},{8,9},{9,8},{10,11... | collective-permute-start | bytes 294920 | tf_op jit(solution)/shard_map/ppermute | solution.py:12
  25.5 1.9 %collective-permute-start.2 = (bf16[2,192,128]{2,1,0:T(8,128)(2,1)S(1)}, bf16[2,192,128]{2,1,0:T(8,128)(2,1)S(1)}, u32[]{:S(2)}, u32[]{:S(2)}) collective-permute-start(bf16[2,192,128]{2,1,0:T(8,128)(2,1)S(1)} %collective-permute-done.1), channel_id=1, source_target_pairs={{0,1},{1,0},{2,3},{3,2},{4,5},{5,4},{6,7},{7,6},{8,9},{9,8},{10,11... | collective-permute-start | bytes 294920 | tf_op jit(solution)/shard_map/ppermute | solution.py:12
  28.5 4.8 %collective-permute-done.5 = bf16[2,192,128]{2,1,0:T(8,128)(2,1)S(1)} collective-permute-done((bf16[2,192,128]{2,1,0:T(8,128)(2,1)S(1)}, bf16[2,192,128]{2,1,0:T(8,128)(2,1)S(1)}, u32[]{:S(2)}, u32[]{:S(2)}) %collective-permute-start.5) | collective-permute-done | bytes 98336 | tf_op jit(solution)/shard_map/ppermute | solution.py:18
  33.3 1.9 %collective-permute-start.6 = (bf16[2,192,128]{2,1,0:T(8,128)(2,1)S(1)}, bf16[2,192,128]{2,1,0:T(8,128)(2,1)S(1)}, u32[]{:S(2)}, u32[]{:S(2)}) collective-permute-start(bf16[2,192,128]{2,1,0:T(8,128)(2,1)S(1)} %collective-permute-done.5), channel_id=1, source_target_pairs={{0,8},{1,9},{2,10},{3,11},{4,12},{5,13},{6,14},{7,15},{8,0},{9,1},... | collective-permute-start | bytes 294920 | tf_op jit(solution)/shard_map/ppermute | solution.py:12
  35.2 2.3 %collective-permute-start.3 = (bf16[2,192,128]{2,1,0:T(8,128)(2,1)S(1)}, bf16[2,192,128]{2,1,0:T(8,128)(2,1)S(1)}, u32[]{:S(2)}, u32[]{:S(2)}) collective-permute-start(bf16[2,192,128]{2,1,0:T(8,128)(2,1)S(1)} %collective-permute-done.2), channel_id=1, source_target_pairs={{0,511},{1,0},{2,1},{3,2},{4,3},{5,4},{6,5},{7,6},{8,7},{9,8},{10,... | collective-permute-start | bytes 294920 | tf_op jit(solution)/shard_map/ppermute | solution.py:18
  37.6 7.7 %collective-permute-done.6 = bf16[2,192,128]{2,1,0:T(8,128)(2,1)S(1)} collective-permute-done((bf16[2,192,128]{2,1,0:T(8,128)(2,1)S(1)}, bf16[2,192,128]{2,1,0:T(8,128)(2,1)S(1)}, u32[]{:S(2)}, u32[]{:S(2)}) %collective-permute-start.6) | collective-permute-done | bytes 98336 | tf_op jit(solution)/shard_map/ppermute | solution.py:12
  45.3 10.4 %collective-permute-start.7 = (bf16[2,192,128]{2,1,0:T(8,128)(2,1)S(1)}, bf16[2,192,128]{2,1,0:T(8,128)(2,1)S(1)}, u32[]{:S(2)}, u32[]{:S(2)}) collective-permute-start(bf16[2,192,128]{2,1,0:T(8,128)(2,1)S(1)} %collective-permute-done.6), channel_id=1, source_target_pairs={{0,504},{1,505},{2,506},{3,507},{4,508},{5,509},{6,510},{7,511},{8... | collective-permute-start | bytes 294920 | tf_op jit(solution)/shard_map/ppermute | solution.py:18
  55.7 3.1 %collective-permute-done.7 = bf16[2,192,128]{2,1,0:T(8,128)(2,1)S(1)} collective-permute-done((bf16[2,192,128]{2,1,0:T(8,128)(2,1)S(1)}, bf16[2,192,128]{2,1,0:T(8,128)(2,1)S(1)}, u32[]{:S(2)}, u32[]{:S(2)}) %collective-permute-start.7) | collective-permute-done | bytes 98336 | tf_op jit(solution)/shard_map/ppermute | solution.py:18
  58.8 4.0 %fusion = f32[2,192,2,1024]{3,1,2,0:T(8,128)S(1)} fusion(bf16[1,2,1024,1024]{3,2,1,0:T(8,128)(2,1)} %param.5, bf16[2,192,1024]{2,1,0:T(8,128)(2,1)S(1)} %constant_dynamic-update-slice_fusion), kind=kOutput, calls=%fused_computation | convolution fusion | flops 1610612736 | bytes 8126464 | tf_op jit(solution)/shard_map/prk,qjk->prqj/dot_general | solution.py:22
  63.3 1.9 %collective-permute-start.9 = (bf16[2,192,128]{2,1,0:T(8,128)(2,1)S(1)}, bf16[2,192,128]{2,1,0:T(8,128)(2,1)S(1)}, u32[]{:S(2)}, u32[]{:S(2)}) collective-permute-start(bf16[2,192,128]{2,1,0:T(8,128)(2,1)S(1)} %get-tuple-element.9), channel_id=1, source_target_pairs={{0,1},{1,2},{2,3},{3,4},{4,5},{5,6},{6,7},{7,8},{8,9},{9,10},{10,1... | collective-permute-start | bytes 294920 | tf_op jit(solution)/shard_map/ppermute | solution.py:18
  67.7 1.9 %collective-permute-start.13 = (bf16[2,192,128]{2,1,0:T(8,128)(2,1)S(1)}, bf16[2,192,128]{2,1,0:T(8,128)(2,1)S(1)}, u32[]{:S(2)}, u32[]{:S(2)}) collective-permute-start(bf16[2,192,128]{2,1,0:T(8,128)(2,1)S(1)} %get-tuple-element.7), channel_id=1, source_target_pairs={{0,8},{1,9},{2,10},{3,11},{4,12},{5,13},{6,14},{7,15},{8,16},{9,17... | collective-permute-start | bytes 294920 | tf_op jit(solution)/shard_map/ppermute | solution.py:18
  69.6 4.0 %collective-permute-start.12 = (bf16[2,192,128]{2,1,0:T(8,128)(2,1)S(1)}, bf16[2,192,128]{2,1,0:T(8,128)(2,1)S(1)}, u32[]{:S(2)}, u32[]{:S(2)}) collective-permute-start(bf16[2,192,128]{2,1,0:T(8,128)(2,1)S(1)} %get-tuple-element.8), channel_id=1, source_target_pairs={{0,8},{1,9},{2,10},{3,11},{4,12},{5,13},{6,14},{7,15},{8,0},{9,1},... | collective-permute-start | bytes 294920 | tf_op jit(solution)/shard_map/ppermute | solution.py:12
  73.6 3.2 %collective-permute-start.8 = (bf16[2,192,128]{2,1,0:T(8,128)(2,1)S(1)}, bf16[2,192,128]{2,1,0:T(8,128)(2,1)S(1)}, u32[]{:S(2)}, u32[]{:S(2)}) collective-permute-start(bf16[2,192,128]{2,1,0:T(8,128)(2,1)S(1)} %get-tuple-element.10), channel_id=1, source_target_pairs={{0,1},{1,0},{2,3},{3,2},{4,5},{5,4},{6,7},{7,6},{8,9},{9,8},{10,11... | collective-permute-start | bytes 294920 | tf_op jit(solution)/shard_map/ppermute | solution.py:12
  76.8 1.9 %collective-permute-start.10 = (bf16[2,192,128]{2,1,0:T(8,128)(2,1)S(1)}, bf16[2,192,128]{2,1,0:T(8,128)(2,1)S(1)}, u32[]{:S(2)}, u32[]{:S(2)}) collective-permute-start(bf16[2,192,128]{2,1,0:T(8,128)(2,1)S(1)} %collective-permute-done.9), channel_id=1, source_target_pairs={{0,1},{1,0},{2,3},{3,2},{4,5},{5,4},{6,7},{7,6},{8,9},{9,8},{10,11... | collective-permute-start | bytes 294920 | tf_op jit(solution)/shard_map/ppermute | solution.py:12
  78.8 5.7 %collective-permute-done.13 = bf16[2,192,128]{2,1,0:T(8,128)(2,1)S(1)} collective-permute-done((bf16[2,192,128]{2,1,0:T(8,128)(2,1)S(1)}, bf16[2,192,128]{2,1,0:T(8,128)(2,1)S(1)}, u32[]{:S(2)}, u32[]{:S(2)}) %collective-permute-start.13) | collective-permute-done | bytes 98336 | tf_op jit(solution)/shard_map/ppermute | solution.py:18
  84.4 1.9 %collective-permute-start.14 = (bf16[2,192,128]{2,1,0:T(8,128)(2,1)S(1)}, bf16[2,192,128]{2,1,0:T(8,128)(2,1)S(1)}, u32[]{:S(2)}, u32[]{:S(2)}) collective-permute-start(bf16[2,192,128]{2,1,0:T(8,128)(2,1)S(1)} %collective-permute-done.13), channel_id=1, source_target_pairs={{0,8},{1,9},{2,10},{3,11},{4,12},{5,13},{6,14},{7,15},{8,0},{9,1},... | collective-permute-start | bytes 294920 | tf_op jit(solution)/shard_map/ppermute | solution.py:12
  86.4 1.9 %collective-permute-start.11 = (bf16[2,192,128]{2,1,0:T(8,128)(2,1)S(1)}, bf16[2,192,128]{2,1,0:T(8,128)(2,1)S(1)}, u32[]{:S(2)}, u32[]{:S(2)}) collective-permute-start(bf16[2,192,128]{2,1,0:T(8,128)(2,1)S(1)} %collective-permute-done.10), channel_id=1, source_target_pairs={{0,511},{1,0},{2,1},{3,2},{4,3},{5,4},{6,5},{7,6},{8,7},{9,8},{10,... | collective-permute-start | bytes 294920 | tf_op jit(solution)/shard_map/ppermute | solution.py:18
  88.4 6.8 %collective-permute-done.14 = bf16[2,192,128]{2,1,0:T(8,128)(2,1)S(1)} collective-permute-done((bf16[2,192,128]{2,1,0:T(8,128)(2,1)S(1)}, bf16[2,192,128]{2,1,0:T(8,128)(2,1)S(1)}, u32[]{:S(2)}, u32[]{:S(2)}) %collective-permute-start.14) | collective-permute-done | bytes 98336 | tf_op jit(solution)/shard_map/ppermute | solution.py:12
  95.2 11.8 %collective-permute-start.15 = (bf16[2,192,128]{2,1,0:T(8,128)(2,1)S(1)}, bf16[2,192,128]{2,1,0:T(8,128)(2,1)S(1)}, u32[]{:S(2)}, u32[]{:S(2)}) collective-permute-start(bf16[2,192,128]{2,1,0:T(8,128)(2,1)S(1)} %collective-permute-done.14), channel_id=1, source_target_pairs={{0,504},{1,505},{2,506},{3,507},{4,508},{5,509},{6,510},{7,511},{8... | collective-permute-start | bytes 294920 | tf_op jit(solution)/shard_map/ppermute | solution.py:18
  107.1 3.0 %collective-permute-done.15 = bf16[2,192,128]{2,1,0:T(8,128)(2,1)S(1)} collective-permute-done((bf16[2,192,128]{2,1,0:T(8,128)(2,1)S(1)}, bf16[2,192,128]{2,1,0:T(8,128)(2,1)S(1)}, u32[]{:S(2)}, u32[]{:S(2)}) %collective-permute-start.15) | collective-permute-done | bytes 98336 | tf_op jit(solution)/shard_map/ppermute | solution.py:18
  (26 shorter events, 5.2 us)
Async XLA Ops:
  9.0 16.5 %collective-permute-start.1 = (bf16[2,192,128]{2,1,0:T(8,128)(2,1)S(1)}, bf16[2,192,128]{2,1,0:T(8,128)(2,1)S(1)}, u32[]{:S(2)}, u32[]{:S(2)}) collective-permute-start(bf16[2,192,128]{2,1,0:T(8,128)(2,1)S(1)} %get-tuple-element.13), channel_id=1, source_target_pairs={{0,1},{1,2},{2,3},{3,4},{4,5},{5,6},{6,7},{7,8},{8,9},{9,10},{10,1... | collective-permute-start | bytes 294920 | tf_op jit(solution)/shard_map/ppermute | solution.py:18
  10.9 22.4 %collective-permute-start.5 = (bf16[2,192,128]{2,1,0:T(8,128)(2,1)S(1)}, bf16[2,192,128]{2,1,0:T(8,128)(2,1)S(1)}, u32[]{:S(2)}, u32[]{:S(2)}) collective-permute-start(bf16[2,192,128]{2,1,0:T(8,128)(2,1)S(1)} %get-tuple-element.11), channel_id=1, source_target_pairs={{0,8},{1,9},{2,10},{3,11},{4,12},{5,13},{6,14},{7,15},{8,16},{9,17... | collective-permute-start | bytes 294920 | tf_op jit(solution)/shard_map/ppermute | solution.py:18
  16.9 38.8 %collective-permute-start.4 = (bf16[2,192,128]{2,1,0:T(8,128)(2,1)S(1)}, bf16[2,192,128]{2,1,0:T(8,128)(2,1)S(1)}, u32[]{:S(2)}, u32[]{:S(2)}) collective-permute-start(bf16[2,192,128]{2,1,0:T(8,128)(2,1)S(1)} %get-tuple-element.12), channel_id=1, source_target_pairs={{0,8},{1,9},{2,10},{3,11},{4,12},{5,13},{6,14},{7,15},{8,0},{9,1},... | collective-permute-start | bytes 294920 | tf_op jit(solution)/shard_map/ppermute | solution.py:12
  22.5 15.1 %collective-permute-start = (bf16[2,192,128]{2,1,0:T(8,128)(2,1)S(1)}, bf16[2,192,128]{2,1,0:T(8,128)(2,1)S(1)}, u32[]{:S(2)}, u32[]{:S(2)}) collective-permute-start(bf16[2,192,128]{2,1,0:T(8,128)(2,1)S(1)} %get-tuple-element.14), channel_id=1, source_target_pairs={{0,1},{1,0},{2,3},{3,2},{4,5},{5,4},{6,7},{7,6},{8,9},{9,8},{10,11... | collective-permute-start | bytes 294920 | tf_op jit(solution)/shard_map/ppermute | solution.py:12
  25.5 9.7 %collective-permute-start.2 = (bf16[2,192,128]{2,1,0:T(8,128)(2,1)S(1)}, bf16[2,192,128]{2,1,0:T(8,128)(2,1)S(1)}, u32[]{:S(2)}, u32[]{:S(2)}) collective-permute-start(bf16[2,192,128]{2,1,0:T(8,128)(2,1)S(1)} %collective-permute-done.1), channel_id=1, source_target_pairs={{0,1},{1,0},{2,3},{3,2},{4,5},{5,4},{6,7},{7,6},{8,9},{9,8},{10,11... | collective-permute-start | bytes 294920 | tf_op jit(solution)/shard_map/ppermute | solution.py:12
  33.3 11.9 %collective-permute-start.6 = (bf16[2,192,128]{2,1,0:T(8,128)(2,1)S(1)}, bf16[2,192,128]{2,1,0:T(8,128)(2,1)S(1)}, u32[]{:S(2)}, u32[]{:S(2)}) collective-permute-start(bf16[2,192,128]{2,1,0:T(8,128)(2,1)S(1)} %collective-permute-done.5), channel_id=1, source_target_pairs={{0,8},{1,9},{2,10},{3,11},{4,12},{5,13},{6,14},{7,15},{8,0},{9,1},... | collective-permute-start | bytes 294920 | tf_op jit(solution)/shard_map/ppermute | solution.py:12
  35.2 20.4 %collective-permute-start.3 = (bf16[2,192,128]{2,1,0:T(8,128)(2,1)S(1)}, bf16[2,192,128]{2,1,0:T(8,128)(2,1)S(1)}, u32[]{:S(2)}, u32[]{:S(2)}) collective-permute-start(bf16[2,192,128]{2,1,0:T(8,128)(2,1)S(1)} %collective-permute-done.2), channel_id=1, source_target_pairs={{0,511},{1,0},{2,1},{3,2},{4,3},{5,4},{6,5},{7,6},{8,7},{9,8},{10,... | collective-permute-start | bytes 294920 | tf_op jit(solution)/shard_map/ppermute | solution.py:18
  45.3 13.6 %collective-permute-start.7 = (bf16[2,192,128]{2,1,0:T(8,128)(2,1)S(1)}, bf16[2,192,128]{2,1,0:T(8,128)(2,1)S(1)}, u32[]{:S(2)}, u32[]{:S(2)}) collective-permute-start(bf16[2,192,128]{2,1,0:T(8,128)(2,1)S(1)} %collective-permute-done.6), channel_id=1, source_target_pairs={{0,504},{1,505},{2,506},{3,507},{4,508},{5,509},{6,510},{7,511},{8... | collective-permute-start | bytes 294920 | tf_op jit(solution)/shard_map/ppermute | solution.py:18
  63.3 13.4 %collective-permute-start.9 = (bf16[2,192,128]{2,1,0:T(8,128)(2,1)S(1)}, bf16[2,192,128]{2,1,0:T(8,128)(2,1)S(1)}, u32[]{:S(2)}, u32[]{:S(2)}) collective-permute-start(bf16[2,192,128]{2,1,0:T(8,128)(2,1)S(1)} %get-tuple-element.9), channel_id=1, source_target_pairs={{0,1},{1,2},{2,3},{3,4},{4,5},{5,6},{6,7},{7,8},{8,9},{9,10},{10,1... | collective-permute-start | bytes 294920 | tf_op jit(solution)/shard_map/ppermute | solution.py:18
  67.7 16.7 %collective-permute-start.13 = (bf16[2,192,128]{2,1,0:T(8,128)(2,1)S(1)}, bf16[2,192,128]{2,1,0:T(8,128)(2,1)S(1)}, u32[]{:S(2)}, u32[]{:S(2)}) collective-permute-start(bf16[2,192,128]{2,1,0:T(8,128)(2,1)S(1)} %get-tuple-element.7), channel_id=1, source_target_pairs={{0,8},{1,9},{2,10},{3,11},{4,12},{5,13},{6,14},{7,15},{8,16},{9,17... | collective-permute-start | bytes 294920 | tf_op jit(solution)/shard_map/ppermute | solution.py:18
  69.6 37.4 %collective-permute-start.12 = (bf16[2,192,128]{2,1,0:T(8,128)(2,1)S(1)}, bf16[2,192,128]{2,1,0:T(8,128)(2,1)S(1)}, u32[]{:S(2)}, u32[]{:S(2)}) collective-permute-start(bf16[2,192,128]{2,1,0:T(8,128)(2,1)S(1)} %get-tuple-element.8), channel_id=1, source_target_pairs={{0,8},{1,9},{2,10},{3,11},{4,12},{5,13},{6,14},{7,15},{8,0},{9,1},... | collective-permute-start | bytes 294920 | tf_op jit(solution)/shard_map/ppermute | solution.py:12
  73.6 14.7 %collective-permute-start.8 = (bf16[2,192,128]{2,1,0:T(8,128)(2,1)S(1)}, bf16[2,192,128]{2,1,0:T(8,128)(2,1)S(1)}, u32[]{:S(2)}, u32[]{:S(2)}) collective-permute-start(bf16[2,192,128]{2,1,0:T(8,128)(2,1)S(1)} %get-tuple-element.10), channel_id=1, source_target_pairs={{0,1},{1,0},{2,3},{3,2},{4,5},{5,4},{6,7},{7,6},{8,9},{9,8},{10,11... | collective-permute-start | bytes 294920 | tf_op jit(solution)/shard_map/ppermute | solution.py:12
  76.8 9.6 %collective-permute-start.10 = (bf16[2,192,128]{2,1,0:T(8,128)(2,1)S(1)}, bf16[2,192,128]{2,1,0:T(8,128)(2,1)S(1)}, u32[]{:S(2)}, u32[]{:S(2)}) collective-permute-start(bf16[2,192,128]{2,1,0:T(8,128)(2,1)S(1)} %collective-permute-done.9), channel_id=1, source_target_pairs={{0,1},{1,0},{2,3},{3,2},{4,5},{5,4},{6,7},{7,6},{8,9},{9,8},{10,11... | collective-permute-start | bytes 294920 | tf_op jit(solution)/shard_map/ppermute | solution.py:12
  84.4 10.8 %collective-permute-start.14 = (bf16[2,192,128]{2,1,0:T(8,128)(2,1)S(1)}, bf16[2,192,128]{2,1,0:T(8,128)(2,1)S(1)}, u32[]{:S(2)}, u32[]{:S(2)}) collective-permute-start(bf16[2,192,128]{2,1,0:T(8,128)(2,1)S(1)} %collective-permute-done.13), channel_id=1, source_target_pairs={{0,8},{1,9},{2,10},{3,11},{4,12},{5,13},{6,14},{7,15},{8,0},{9,1},... | collective-permute-start | bytes 294920 | tf_op jit(solution)/shard_map/ppermute | solution.py:12
  86.4 20.6 %collective-permute-start.11 = (bf16[2,192,128]{2,1,0:T(8,128)(2,1)S(1)}, bf16[2,192,128]{2,1,0:T(8,128)(2,1)S(1)}, u32[]{:S(2)}, u32[]{:S(2)}) collective-permute-start(bf16[2,192,128]{2,1,0:T(8,128)(2,1)S(1)} %collective-permute-done.10), channel_id=1, source_target_pairs={{0,511},{1,0},{2,1},{3,2},{4,3},{5,4},{6,5},{7,6},{8,7},{9,8},{10,... | collective-permute-start | bytes 294920 | tf_op jit(solution)/shard_map/ppermute | solution.py:18
  95.2 14.9 %collective-permute-start.15 = (bf16[2,192,128]{2,1,0:T(8,128)(2,1)S(1)}, bf16[2,192,128]{2,1,0:T(8,128)(2,1)S(1)}, u32[]{:S(2)}, u32[]{:S(2)}) collective-permute-start(bf16[2,192,128]{2,1,0:T(8,128)(2,1)S(1)} %collective-permute-done.14), channel_id=1, source_target_pairs={{0,504},{1,505},{2,506},{3,507},{4,508},{5,509},{6,510},{7,511},{8... | collective-permute-start | bytes 294920 | tf_op jit(solution)/shard_map/ppermute | solution.py:18
where the time goes:
time: 112 us; the launch traced here: 111 us
  starting transfers between devices  61.5 us (55%)
  waiting for transfers between devices  31.1 us (28%)
  between operations  7.71 us (7%)
  local copies, waits for them, and re-layouts  4.1 us (4%)
  matrix products  4.01 us (4%)
  other arithmetic  2.58 us (2%)
    ppermute x8, starting transfers between devices, passed_along(): return lax.ppermute(value, axis, pairs)  38.1 us
    ppermute x8, starting transfers between devices, from_partner(): lax.ppermute(value, axis, [(i, i ^ 1 << distance) for i in range(lax.axis...  23.4 us
    ppermute x8, waiting for transfers between devices, passed_along(): return lax.ppermute(value, axis, pairs)  16.6 us
    ppermute x8, waiting for transfers between devices, from_partner(): lax.ppermute(value, axis, [(i, i ^ 1 << distance) for i in range(lax.axis...  14.5 us
    dot_general x1, matrix products, complex_apply(): jnp.einsum('prk,qjk->prqj', values, matrix, preferred_element_type=jnp.fl...  4.01 us
  transfers between devices with their start and end apart: 16, of which 6 were waited for; matrix products, arithmetic and copies ran while one was open for 1% of the time, Pallas kernels for 0%

commit v1 on v0

v1 whole, which is shorter than its diff:
```python
import functools

import jax
import jax.numpy as jnp
from jax import lax
from jax.experimental import pallas as pl
from jax.experimental.pallas import tpu as pltpu
from jax.sharding import PartitionSpec as P

MESH = pl.DeviceIdType.MESH
BLK = 128
COLS = 8
OWN = 512
ORDER = 1024
RHS = 192
ROUNDS = 4
CHUNKS = 2
RC = RHS // CHUNKS
SEND_ORDER = (3, 2, 1, 0)


def partners(me, count):
    column_odd = lax.rem(me, 2)
    line_odd = lax.rem(me // COLS, 2)
    steps = (
        1 - 2 * column_odd,
        2 * column_odd - 1,
        COLS * (1 - 2 * line_odd),
        COLS * (2 * line_odd - 1),
    )
    return [lax.rem(me + step + count, count) for step in steps]


def kernel(
    count,
    blk_ref,
    flg_ref,
    cur_hbm,
    inv_hbm,
    out_hbm,
    cur,
    mat,
    own,
    slot,
    local,
    lend,
    lent,
    back,
    arrived,
    out,
    load_sem,
    lend_send,
    lend_recv,
    back_send,
    back_recv,
):
    me = lax.axis_index("groups")
    partner = partners(me, count)

    load_cur = pltpu.make_async_copy(cur_hbm, cur, load_sem.at[0])
    load_cur.start()
    barrier = pltpu.get_barrier_semaphore()
    for r in SEND_ORDER:
        pl.semaphore_signal(barrier, inc=1, device_id=(partner[r],), device_id_type=MESH)
    load_mat = []
    for half in range(2):
        for part in range(2):
            load_mat.append(
                pltpu.make_async_copy(
                    inv_hbm.at[0, part, :, pl.ds(half * OWN, OWN)],
                    mat.at[:, pl.ds(half * ORDER + part * OWN, OWN)],
                    load_sem.at[1 + 2 * half + part],
                )
            )
            load_mat[-1].start()

    weight = [
        [
            jnp.where(blk_ref[0, r] == b, flg_ref[0, r], 0).astype(jnp.float32)
            for b in range(OWN // BLK)
        ]
        for r in range(ROUNDS)
    ]
    load_cur.wait()
    for r in range(ROUNDS):
        for c in range(CHUNKS):
            piece = jnp.zeros((2, RC, BLK), jnp.bfloat16)
            for b in range(OWN // BLK):
                block = cur[:, pl.ds(c * RC, RC), pl.ds(b * BLK, BLK)]
                piece += block * weight[r][b].astype(jnp.bfloat16)
            lend[c, r] = piece

    pl.semaphore_wait(barrier, ROUNDS)

    def remote(src, dst, send, recv, c, r):
        return pltpu.make_async_remote_copy(
            src_ref=src.at[c, r],
            dst_ref=dst.at[c, r],
            send_sem=send.at[c, r],
            recv_sem=recv.at[c, r],
            device_id=(partner[r],),
            device_id_type=MESH,
        )

    lends = {}
    for c in range(CHUNKS):
        for r in SEND_ORDER:
            lends[c, r] = remote(lend, lent, lend_send, lend_recv, c, r)
            lends[c, r].start()

    for c in range(CHUNKS):
        real = cur[0, pl.ds(c * RC, RC), :]
        imag = cur[1, pl.ds(c * RC, RC), :]
        own[c, 0, :, pl.ds(0, OWN)] = real
        own[c, 0, :, pl.ds(OWN, OWN)] = -imag
        own[c, 1, :, pl.ds(0, OWN)] = imag
        own[c, 1, :, pl.ds(OWN, OWN)] = real

    def product(rows, matrix):
        return lax.dot_general(
            rows, matrix, (((1,), (1,)), ((), ())), preferred_element_type=jnp.float32
        )

    load_mat[0].wait()
    load_mat[1].wait()
    own_rows = own[...].reshape(2 * RHS, ORDER)
    for half in (1, 0):
        rows = pl.ds(half * OWN, OWN)
        local[:, :, :, rows] = product(own_rows, mat[rows, pl.ds(0, ORDER)]).reshape(
            CHUNKS, 2, RC, OWN
        )
    load_mat[2].wait()
    load_mat[3].wait()

    backs = {}
    for c in range(CHUNKS):
        for r in SEND_ORDER:
            lends[c, r].wait_recv()
            real = lent[c, r, 0]
            imag = lent[c, r, 1]
            slot[c, 0, :, pl.ds(r * BLK, BLK)] = real
            slot[c, 0, :, pl.ds(OWN + r * BLK, BLK)] = -imag
            slot[c, 1, :, pl.ds(r * BLK, BLK)] = imag
            slot[c, 1, :, pl.ds(OWN + r * BLK, BLK)] = real
        slot_rows = slot[c].reshape(2 * RC, ORDER)
        far = pl.ds(OWN, OWN)
        returned = local[c, :, :, far] + product(
            slot_rows, mat[far, pl.ds(ORDER, ORDER)]
        ).reshape(2, RC, OWN)
        for r in SEND_ORDER:
            back[c, r] = returned[:, :, r * BLK : (r + 1) * BLK].astype(jnp.bfloat16)
            backs[c, r] = remote(back, arrived, back_send, back_recv, c, r)
            backs[c, r].start()
        near = pl.ds(0, OWN)
        local[c, :, :, near] += product(slot_rows, mat[near, pl.ds(ORDER, ORDER)]).reshape(
            2, RC, OWN
        )

    stores = []
    for c in range(CHUNKS):
        for r in SEND_ORDER:
            backs[c, r].wait_recv()
        for b in range(OWN // BLK):
            total = local[c, :, :, pl.ds(b * BLK, BLK)]
            for r in range(ROUNDS):
                total += arrived[c, r].astype(jnp.float32) * weight[r][b]
            out[:, pl.ds(c * RC, RC), pl.ds(b * BLK, BLK)] = total.astype(jnp.bfloat16)
        stores.append(
            pltpu.make_async_copy(
                out.at[:, pl.ds(c * RC, RC), :],
                out_hbm.at[:, pl.ds(c * RC, RC), :],
                load_sem.at[5 + c],
            )
        )
        stores[-1].start()
    for copy in stores:
        copy.wait()
    for c in range(CHUNKS):
        for r in range(ROUNDS):
            lends[c, r].wait_send()
            backs[c, r].wait_send()


def solution(mesh):
    count = mesh.shape["groups"]

    def step(currents, inverse, send_blocks, send_flags):
        pieces = (CHUNKS, ROUNDS, 2, RC, BLK)
        return pl.pallas_call(
            functools.partial(kernel, count),
            out_shape=jax.ShapeDtypeStruct(currents.shape, jnp.bfloat16),
            in_specs=[
                pl.BlockSpec(memory_space=pltpu.SMEM),
                pl.BlockSpec(memory_space=pltpu.SMEM),
                pl.BlockSpec(memory_space=pl.ANY),
                pl.BlockSpec(memory_space=pl.ANY),
            ],
            out_specs=pl.BlockSpec(memory_space=pl.ANY),
            scratch_shapes=[
                pltpu.VMEM((2, RHS, OWN), jnp.bfloat16),
                pltpu.VMEM((ORDER, 2 * ORDER), jnp.bfloat16),
                pltpu.VMEM((CHUNKS, 2, RC, ORDER), jnp.bfloat16),
                pltpu.VMEM((CHUNKS, 2, RC, ORDER), jnp.bfloat16),
                pltpu.VMEM((CHUNKS, 2, RC, ORDER), jnp.float32),
                pltpu.VMEM(pieces, jnp.bfloat16),
                pltpu.VMEM(pieces, jnp.bfloat16),
                pltpu.VMEM(pieces, jnp.bfloat16),
                pltpu.VMEM(pieces, jnp.bfloat16),
                pltpu.VMEM((2, RHS, OWN), jnp.bfloat16),
                pltpu.SemaphoreType.DMA((5 + CHUNKS,)),
                pltpu.SemaphoreType.DMA((CHUNKS, ROUNDS)),
                pltpu.SemaphoreType.DMA((CHUNKS, ROUNDS)),
                pltpu.SemaphoreType.DMA((CHUNKS, ROUNDS)),
                pltpu.SemaphoreType.DMA((CHUNKS, ROUNDS)),
            ],
            compiler_params=pltpu.CompilerParams(
                collective_id=1,
                has_side_effects=True,
                vmem_limit_bytes=60 * 1024 * 1024,
            ),
            cost_estimate=pl.CostEstimate(
                flops=8 * RHS * ORDER * ORDER,
                bytes_accessed=4 * ORDER * ORDER + 8 * RHS * OWN,
                transcendentals=0,
            ),
        )(send_blocks, send_flags, currents, inverse)

    in_specs = (
        P(None, None, "groups"),
        P("groups", None, None, None),
        P("groups", None),
        P("groups", None),
    )
    return jax.shard_map(
        step, mesh=mesh, in_specs=in_specs, out_specs=P(None, None, "groups"), check_vma=False
    )
```

time: 112 us -> 46.1 us (0.41)
  the two profiles are of different devices: /device:TPU:16 before, /device:TPU:8 now
where the time goes in v1:
time: 46.1 us; the launch traced here: 46 us
  Pallas kernels  44.2 us (96%)
  local copies, waits for them, and re-layouts  1.77 us (4%)
    pallas_call x1, Pallas kernels, step(): pl.pallas_call(functools.partial(kernel, count), out_shape=jax.ShapeDtype...  44.2 us
    unnamed x1, local copies, waits for them, and re-layouts  1.77 us

profile of v1, /device:TPU:8, one launch (start us, length us, event | category | flops | bytes accessed | tf_op | source)
XLA Modules:
  0.0 46.0 jit_solution(4330320174132618062)
XLA Ops:
  0.0 44.2 %shard_map.46 = bf16[2,192,512]{2,1,0:T(8,128)(2,1)} custom-call(s32[1,4]{1,0:T(1,128)} %blk_ref.1, s32[1,4]{1,0:T(1,128)} %flg_ref.1, bf16[2,192,512]{2,1,0:T(8,128)(2,1)} %cur_hbm.1, bf16[1,2,1024,1024]{3,2,1,0:T(8,128)(2,1)} %inv_hbm.1), custom_call_target="tpu_custom_call" | custom-call | flops 1610612736 | bytes 4980736 | tf_op jit(solution)/shard_map/pallas_call | solution.py:189
  44.2 1.8 %copy.6 = bf16[2,192,512]{2,1,0:T(8,128)(2,1)} copy(bf16[2,192,512]{2,1,0:T(8,128)(2,1)} %shard_map.46) | data formatting | bytes 786432

commit v2 on v1

--- a/solution.py
+++ b/solution.py
@@ -14,6 +14,7 @@
 ORDER = 1024
 RHS = 192
 ROUNDS = 4
+PLANE = 128
 CHUNKS = 2
 RC = RHS // CHUNKS
 SEND_ORDER = (3, 2, 1, 0)
@@ -31,13 +32,21 @@
     return [lax.rem(me + step + count, count) for step in steps]
 
 
+def ends(me):
+    line = lax.rem(me // COLS, PLANE // COLS)
+    column = lax.rem(me, PLANE)
+    first = (None, column == 0, None, line == 0)
+    last = (None, column == PLANE - 1, None, line == PLANE // COLS - 1)
+    return first, last
+
+
 def kernel(
     count,
     blk_ref,
     flg_ref,
     cur_hbm,
     inv_hbm,
-    out_hbm,
+    out,
     cur,
     mat,
     own,
@@ -47,12 +56,12 @@
     lent,
     back,
     arrived,
-    out,
     load_sem,
     lend_send,
     lend_recv,
     back_send,
     back_recv,
+    ready,
 ):
     me = lax.axis_index("groups")
     partner = partners(me, count)
@@ -60,8 +69,19 @@
     load_cur = pltpu.make_async_copy(cur_hbm, cur, load_sem.at[0])
     load_cur.start()
     barrier = pltpu.get_barrier_semaphore()
+    first, last = ends(me)
+
+    def greet(r):
+        pl.semaphore_signal(barrier, inc=1, device_id=(partner[r],), device_id_type=MESH)
+
+    def unless(condition, do):
+        if condition is None:
+            do()
+        else:
+            pl.when(jnp.logical_not(condition))(do)
+
     for r in SEND_ORDER:
-        pl.semaphore_signal(barrier, inc=1, device_id=(partner[r],), device_id_type=MESH)
+        unless(last[r], functools.partial(greet, r))
     load_mat = []
     for half in range(2):
         for part in range(2):
@@ -90,7 +110,17 @@
                 piece += block * weight[r][b].astype(jnp.bfloat16)
             lend[c, r] = piece
 
-    pl.semaphore_wait(barrier, ROUNDS)
+    greeted = ROUNDS
+    for r in (1, 3):
+        greeted = greeted - first[r].astype(jnp.int32)
+    pl.semaphore_wait(barrier, greeted)
+    for r in (3, 1):
+
+        @pl.when(last[r])
+        def _():
+            pl.semaphore_signal(
+                ready.at[r], inc=1, device_id=(partner[r],), device_id_type=MESH
+            )
 
     def remote(src, dst, send, recv, c, r):
         return pltpu.make_async_remote_copy(
@@ -106,7 +136,7 @@
     for c in range(CHUNKS):
         for r in SEND_ORDER:
             lends[c, r] = remote(lend, lent, lend_send, lend_recv, c, r)
-            lends[c, r].start()
+            unless(first[r], lends[c, r].start)
 
     for c in range(CHUNKS):
         real = cur[0, pl.ds(c * RC, RC), :]
@@ -131,6 +161,13 @@
         )
     load_mat[2].wait()
     load_mat[3].wait()
+    for r in (3, 1):
+
+        @pl.when(first[r])
+        def _():
+            pl.semaphore_wait(ready.at[r], 1)
+            for c in range(CHUNKS):
+                lends[c, r].start()
 
     backs = {}
     for c in range(CHUNKS):
@@ -150,13 +187,23 @@
         for r in SEND_ORDER:
             back[c, r] = returned[:, :, r * BLK : (r + 1) * BLK].astype(jnp.bfloat16)
             backs[c, r] = remote(back, arrived, back_send, back_recv, c, r)
-            backs[c, r].start()
+            if r == 3:
+                backs[c, r].start()
+            else:
+                unless(last[3], backs[c, r].start)
         near = pl.ds(0, OWN)
         local[c, :, :, near] += product(slot_rows, mat[near, pl.ds(ORDER, ORDER)]).reshape(
             2, RC, OWN
         )
 
-    stores = []
+    @pl.when(last[3])
+    def _():
+        for c in range(CHUNKS):
+            backs[c, 3].wait_send()
+        for r in (2, 1, 0):
+            for c in range(CHUNKS):
+                backs[c, r].start()
+
     for c in range(CHUNKS):
         for r in SEND_ORDER:
             backs[c, r].wait_recv()
@@ -165,20 +212,13 @@
             for r in range(ROUNDS):
                 total += arrived[c, r].astype(jnp.float32) * weight[r][b]
             out[:, pl.ds(c * RC, RC), pl.ds(b * BLK, BLK)] = total.astype(jnp.bfloat16)
-        stores.append(
-            pltpu.make_async_copy(
-                out.at[:, pl.ds(c * RC, RC), :],
-                out_hbm.at[:, pl.ds(c * RC, RC), :],
-                load_sem.at[5 + c],
-            )
-        )
-        stores[-1].start()
-    for copy in stores:
-        copy.wait()
     for c in range(CHUNKS):
         for r in range(ROUNDS):
             lends[c, r].wait_send()
-            backs[c, r].wait_send()
+            if r == 3:
+                unless(last[3], backs[c, r].wait_send)
+            else:
+                backs[c, r].wait_send()
 
 
 def solution(mesh):
@@ -188,14 +228,14 @@
         pieces = (CHUNKS, ROUNDS, 2, RC, BLK)
         return pl.pallas_call(
             functools.partial(kernel, count),
-            out_shape=jax.ShapeDtypeStruct(currents.shape, jnp.bfloat16),
+            out_shape=pltpu.VMEM(currents.shape, jnp.bfloat16),
             in_specs=[
                 pl.BlockSpec(memory_space=pltpu.SMEM),
                 pl.BlockSpec(memory_space=pltpu.SMEM),
                 pl.BlockSpec(memory_space=pl.ANY),
                 pl.BlockSpec(memory_space=pl.ANY),
             ],
-            out_specs=pl.BlockSpec(memory_space=pl.ANY),
+            out_specs=pl.BlockSpec(memory_space=pltpu.VMEM),
             scratch_shapes=[
                 pltpu.VMEM((2, RHS, OWN), jnp.bfloat16),
                 pltpu.VMEM((ORDER, 2 * ORDER), jnp.bfloat16),
@@ -206,12 +246,12 @@
                 pltpu.VMEM(pieces, jnp.bfloat16),
                 pltpu.VMEM(pieces, jnp.bfloat16),
                 pltpu.VMEM(pieces, jnp.bfloat16),
-                pltpu.VMEM((2, RHS, OWN), jnp.bfloat16),
-                pltpu.SemaphoreType.DMA((5 + CHUNKS,)),
-                pltpu.SemaphoreType.DMA((CHUNKS, ROUNDS)),
-                pltpu.SemaphoreType.DMA((CHUNKS, ROUNDS)),
-                pltpu.SemaphoreType.DMA((CHUNKS, ROUNDS)),
-                pltpu.SemaphoreType.DMA((CHUNKS, ROUNDS)),
+                pltpu.SemaphoreType.DMA((5,)),
+                pltpu.SemaphoreType.DMA((CHUNKS, ROUNDS)),
+                pltpu.SemaphoreType.DMA((CHUNKS, ROUNDS)),
+                pltpu.SemaphoreType.DMA((CHUNKS, ROUNDS)),
+                pltpu.SemaphoreType.DMA((CHUNKS, ROUNDS)),
+                pltpu.SemaphoreType.REGULAR((ROUNDS,)),
             ],
             compiler_params=pltpu.CompilerParams(
                 collective_id=1,

time: 46.1 us -> 40.1 us (0.87)
  the two profiles are of different devices: /device:TPU:8 before, /device:TPU:6 now
where the time goes in v2:
time: 40.1 us; the launch traced here: 39.9 us
  Pallas kernels  39.2 us (98%)
  local copies, waits for them, and re-layouts  0.75 us (2%)
    pallas_call x1, Pallas kernels, step(): pl.pallas_call(functools.partial(kernel, count), out_shape=pltpu.VMEM(cur...  39.2 us

profile of v2, /device:TPU:6, one launch (start us, length us, event | category | flops | bytes accessed | tf_op | source)
XLA Modules:
  0.0 39.9 jit_solution(18070353691434573021)
XLA Ops:
  0.0 39.2 %shard_map.46 = bf16[2,192,512]{2,1,0:T(8,128)(2,1)S(1)} custom-call(s32[1,4]{1,0:T(1,128)} %blk_ref.1, s32[1,4]{1,0:T(1,128)} %flg_ref.1, bf16[2,192,512]{2,1,0:T(8,128)(2,1)} %cur_hbm.1, bf16[1,2,1024,1024]{3,2,1,0:T(8,128)(2,1)} %inv_hbm.1), custom_call_target="tpu_custom_call" | custom-call | flops 1610612736 | bytes 4980736 | tf_op jit(solution)/shard_map/pallas_call | solution.py:229
  39.2 0.7 %copy.6 = bf16[2,192,512]{2,1,0:T(8,128)(2,1)} copy(bf16[2,192,512]{2,1,0:T(8,128)(2,1)S(1)} %shard_map.46) | data formatting | bytes 786432

commit v3 on v2

--- a/solution.py
+++ b/solution.py
@@ -62,6 +62,10 @@
     back_send,
     back_recv,
     ready,
+    edge,
+    wedge,
+    wedge_send,
+    wedge_recv,
 ):
     me = lax.axis_index("groups")
     partner = partners(me, count)
@@ -132,11 +136,21 @@
             device_id_type=MESH,
         )
 
+    gives = last[3] & (lax.rem(me, PLANE) != PLANE - COLS)
+    takes = first[3] & (lax.rem(me, PLANE) != 0)
     lends = {}
     for c in range(CHUNKS):
+        for r in range(ROUNDS):
+            lends[c, r] = remote(lend, lent, lend_send, lend_recv, c, r)
+    plane_end = lax.rem(me // COLS, PLANE // COLS) == PLANE // COLS - 2
+    for c in range(CHUNKS):
         for r in SEND_ORDER:
-            lends[c, r] = remote(lend, lent, lend_send, lend_recv, c, r)
-            unless(first[r], lends[c, r].start)
+            if r == 3:
+                pl.when(jnp.logical_not(first[3] | plane_end))(lends[c, r].start)
+            else:
+                unless(first[r], lends[c, r].start)
+    for c in range(CHUNKS):
+        pl.when(plane_end)(lends[c, 3].start)
 
     for c in range(CHUNKS):
         real = cur[0, pl.ds(c * RC, RC), :]
@@ -161,7 +175,7 @@
         )
     load_mat[2].wait()
     load_mat[3].wait()
-    for r in (3, 1):
+    for r in (1, 3):
 
         @pl.when(first[r])
         def _():
@@ -169,28 +183,75 @@
             for c in range(CHUNKS):
                 lends[c, r].start()
 
+    corner = pltpu.make_async_remote_copy(
+        src_ref=edge,
+        dst_ref=wedge,
+        send_sem=wedge_send,
+        recv_sem=wedge_recv,
+        device_id=(partner[3],),
+        device_id_type=MESH,
+    )
+
+    def fill(c, r):
+        lends[c, r].wait_recv()
+        real = lent[c, r, 0]
+        imag = lent[c, r, 1]
+        slot[c, 0, :, pl.ds(r * BLK, BLK)] = real
+        slot[c, 0, :, pl.ds(OWN + r * BLK, BLK)] = -imag
+        slot[c, 1, :, pl.ds(r * BLK, BLK)] = imag
+        slot[c, 1, :, pl.ds(OWN + r * BLK, BLK)] = real
+
     backs = {}
     for c in range(CHUNKS):
-        for r in SEND_ORDER:
-            lends[c, r].wait_recv()
-            real = lent[c, r, 0]
-            imag = lent[c, r, 1]
-            slot[c, 0, :, pl.ds(r * BLK, BLK)] = real
-            slot[c, 0, :, pl.ds(OWN + r * BLK, BLK)] = -imag
-            slot[c, 1, :, pl.ds(r * BLK, BLK)] = imag
-            slot[c, 1, :, pl.ds(OWN + r * BLK, BLK)] = real
+        for r in range(ROUNDS):
+            backs[c, r] = remote(back, arrived, back_send, back_recv, c, r)
+
+    @pl.when(gives)
+    def _():
+        tail = pl.ds(ORDER - BLK, BLK)
+        for part in range(2):
+            edge[:, pl.ds(part * BLK, BLK)] = mat[tail, pl.ds(ORDER + (1 + part) * OWN - BLK, BLK)]
+        corner.start()
+        for c in range(CHUNKS):
+            for r in (0, 1, 2):
+                fill(c, r)
+            part = local[c, :, :, tail].reshape(2 * RC, BLK)
+            for half in range(2):
+                part += product(
+                    slot[c, :, :, pl.ds(half * OWN, OWN - BLK)].reshape(2 * RC, OWN - BLK),
+                    mat[tail, pl.ds(ORDER + half * OWN, OWN - BLK)],
+                )
+            back[c, 3] = part.reshape(2, RC, BLK).astype(jnp.bfloat16)
+            backs[c, 3].start()
+
+    for c in range(CHUNKS):
+
+        @pl.when(jnp.logical_not(gives))
+        def _():
+            for r in (0, 1, 2):
+                fill(c, r)
+
+        fill(c, 3)
         slot_rows = slot[c].reshape(2 * RC, ORDER)
         far = pl.ds(OWN, OWN)
         returned = local[c, :, :, far] + product(
             slot_rows, mat[far, pl.ds(ORDER, ORDER)]
         ).reshape(2, RC, OWN)
         for r in SEND_ORDER:
-            back[c, r] = returned[:, :, r * BLK : (r + 1) * BLK].astype(jnp.bfloat16)
-            backs[c, r] = remote(back, arrived, back_send, back_recv, c, r)
+            piece = returned[:, :, r * BLK : (r + 1) * BLK].astype(jnp.bfloat16)
             if r == 3:
-                backs[c, r].start()
+
+                @pl.when(jnp.logical_not(gives))
+                def _():
+                    back[c, r] = piece
+                    backs[c, r].start()
+
             else:
-                unless(last[3], backs[c, r].start)
+                back[c, r] = piece
+                if r == 1:
+                    pl.when(last[1] | jnp.logical_not(last[3]))(backs[c, r].start)
+                else:
+                    unless(last[3], backs[c, r].start)
         near = pl.ds(0, OWN)
         local[c, :, :, near] += product(slot_rows, mat[near, pl.ds(ORDER, ORDER)]).reshape(
             2, RC, OWN
@@ -202,7 +263,24 @@
             backs[c, 3].wait_send()
         for r in (2, 1, 0):
             for c in range(CHUNKS):
-                backs[c, r].start()
+                unless(last[1] if r == 1 else None, backs[c, r].start)
+
+    @pl.when(takes)
+    def _():
+        corner.wait_recv()
+        for c in range(CHUNKS):
+            real = lend[c, 3, 0]
+            imag = lend[c, 3, 1]
+            mine = jnp.concatenate(
+                [
+                    jnp.concatenate([real, -imag], axis=1),
+                    jnp.concatenate([imag, real], axis=1),
+                ],
+                axis=0,
+            )
+            extra = product(mine, wedge[...]).reshape(2, RC, BLK)
+            for b in range(OWN // BLK):
+                local[c, :, :, pl.ds(b * BLK, BLK)] += extra * weight[3][b]
 
     for c in range(CHUNKS):
         for r in SEND_ORDER:
@@ -212,6 +290,10 @@
             for r in range(ROUNDS):
                 total += arrived[c, r].astype(jnp.float32) * weight[r][b]
             out[:, pl.ds(c * RC, RC), pl.ds(b * BLK, BLK)] = total.astype(jnp.bfloat16)
+    @pl.when(gives)
+    def _():
+        corner.wait_send()
+
     for c in range(CHUNKS):
         for r in range(ROUNDS):
             lends[c, r].wait_send()
@@ -252,6 +334,10 @@
                 pltpu.SemaphoreType.DMA((CHUNKS, ROUNDS)),
                 pltpu.SemaphoreType.DMA((CHUNKS, ROUNDS)),
                 pltpu.SemaphoreType.REGULAR((ROUNDS,)),
+                pltpu.VMEM((BLK, 2 * BLK), jnp.bfloat16),
+                pltpu.VMEM((BLK, 2 * BLK), jnp.bfloat16),
+                pltpu.SemaphoreType.DMA,
+                pltpu.SemaphoreType.DMA,
             ],
             compiler_params=pltpu.CompilerParams(
                 collective_id=1,

time: 40.1 us -> 38.1 us (0.950)
  the two profiles are of different devices: /device:TPU:6 before, /device:TPU:1 now
where the time goes in v3:
time: 38.1 us; the launch traced here: 37.4 us
  Pallas kernels  36.6 us (96%)
  local copies, waits for them, and re-layouts  0.75 us (2%)
    pallas_call x1, Pallas kernels, step(): pl.pallas_call(functools.partial(kernel, count), out_shape=pltpu.VMEM(cur...  36.6 us

profile of v3, /device:TPU:1, one launch (start us, length us, event | category | flops | bytes accessed | tf_op | source)
XLA Modules:
  0.0 37.4 jit_solution(2885519309205101428)
XLA Ops:
  0.0 36.6 %shard_map.46 = bf16[2,192,512]{2,1,0:T(8,128)(2,1)S(1)} custom-call(s32[1,4]{1,0:T(1,128)} %blk_ref.1, s32[1,4]{1,0:T(1,128)} %flg_ref.1, bf16[2,192,512]{2,1,0:T(8,128)(2,1)} %cur_hbm.1, bf16[1,2,1024,1024]{3,2,1,0:T(8,128)(2,1)} %inv_hbm.1), custom_call_target="tpu_custom_call" | custom-call | flops 1610612736 | bytes 4980736 | tf_op jit(solution)/shard_map/pallas_call | solution.py:311
  36.6 0.7 %copy.6 = bf16[2,192,512]{2,1,0:T(8,128)(2,1)} copy(bf16[2,192,512]{2,1,0:T(8,128)(2,1)S(1)} %shard_map.46) | data formatting | bytes 786432

commit v4 on v3

--- a/solution.py
+++ b/solution.py
@@ -37,7 +37,7 @@
     column = lax.rem(me, PLANE)
     first = (None, column == 0, None, line == 0)
     last = (None, column == PLANE - 1, None, line == PLANE // COLS - 1)
-    return first, last
+    return first, last, line == 1
 
 
 def kernel(
@@ -62,6 +62,9 @@
     back_send,
     back_recv,
     ready,
+    relay,
+    relay_send,
+    relay_recv,
     edge,
     wedge,
     wedge_send,
@@ -73,7 +76,9 @@
     load_cur = pltpu.make_async_copy(cur_hbm, cur, load_sem.at[0])
     load_cur.start()
     barrier = pltpu.get_barrier_semaphore()
-    first, last = ends(me)
+    first, last, hub = ends(me)
+    before = lax.rem(me + count - 2 * COLS, count)
+    after = lax.rem(me + 2 * COLS, count)
 
     def greet(r):
         pl.semaphore_signal(barrier, inc=1, device_id=(partner[r],), device_id_type=MESH)
@@ -86,6 +91,11 @@
 
     for r in SEND_ORDER:
         unless(last[r], functools.partial(greet, r))
+
+    @pl.when(hub)
+    def _():
+        pl.semaphore_signal(barrier, inc=1, device_id=(before,), device_id_type=MESH)
+
     load_mat = []
     for half in range(2):
         for part in range(2):
@@ -117,7 +127,7 @@
     greeted = ROUNDS
     for r in (1, 3):
         greeted = greeted - first[r].astype(jnp.int32)
-    pl.semaphore_wait(barrier, greeted)
+    pl.semaphore_wait(barrier, greeted + last[3].astype(jnp.int32))
     for r in (3, 1):
 
         @pl.when(last[r])
@@ -136,17 +146,41 @@
             device_id_type=MESH,
         )
 
-    gives = last[3] & (lax.rem(me, PLANE) != PLANE - COLS)
-    takes = first[3] & (lax.rem(me, PLANE) != 0)
+    gives = last[3]
+    takes = first[3]
     lends = {}
     for c in range(CHUNKS):
         for r in range(ROUNDS):
             lends[c, r] = remote(lend, lent, lend_send, lend_recv, c, r)
+    legs = []
+    for c in range(CHUNKS):
+        legs.append(
+            (
+                pltpu.make_async_remote_copy(
+                    src_ref=lend.at[c, 3],
+                    dst_ref=relay.at[c],
+                    send_sem=lend_send.at[c, 3],
+                    recv_sem=relay_recv.at[c],
+                    device_id=(after,),
+                    device_id_type=MESH,
+                ),
+                pltpu.make_async_remote_copy(
+                    src_ref=relay.at[c],
+                    dst_ref=lent.at[c, 3],
+                    send_sem=relay_send.at[c],
+                    recv_sem=lend_recv.at[c, 3],
+                    device_id=(partner[2],),
+                    device_id_type=MESH,
+                ),
+            )
+        )
+    for c in range(CHUNKS):
+        pl.when(last[3])(legs[c][0].start)
     plane_end = lax.rem(me // COLS, PLANE // COLS) == PLANE // COLS - 2
     for c in range(CHUNKS):
         for r in SEND_ORDER:
             if r == 3:
-                pl.when(jnp.logical_not(first[3] | plane_end))(lends[c, r].start)
+                pl.when(jnp.logical_not(first[3] | last[3] | plane_end))(lends[c, r].start)
             else:
                 unless(first[r], lends[c, r].start)
     for c in range(CHUNKS):
@@ -175,6 +209,12 @@
         )
     load_mat[2].wait()
     load_mat[3].wait()
+    @pl.when(hub)
+    def _():
+        for c in range(CHUNKS):
+            legs[c][0].wait_recv()
+            legs[c][1].start()
+
     for r in (1, 3):
 
         @pl.when(first[r])
@@ -237,7 +277,7 @@
         returned = local[c, :, :, far] + product(
             slot_rows, mat[far, pl.ds(ORDER, ORDER)]
         ).reshape(2, RC, OWN)
-        for r in SEND_ORDER:
+        for r in (2, 1, 0, 3):
             piece = returned[:, :, r * BLK : (r + 1) * BLK].astype(jnp.bfloat16)
             if r == 3:
 
@@ -290,6 +330,11 @@
             for r in range(ROUNDS):
                 total += arrived[c, r].astype(jnp.float32) * weight[r][b]
             out[:, pl.ds(c * RC, RC), pl.ds(b * BLK, BLK)] = total.astype(jnp.bfloat16)
+    @pl.when(hub)
+    def _():
+        for c in range(CHUNKS):
+            legs[c][1].wait_send()
+
     @pl.when(gives)
     def _():
         corner.wait_send()
@@ -334,6 +379,9 @@
                 pltpu.SemaphoreType.DMA((CHUNKS, ROUNDS)),
                 pltpu.SemaphoreType.DMA((CHUNKS, ROUNDS)),
                 pltpu.SemaphoreType.REGULAR((ROUNDS,)),
+                pltpu.VMEM((CHUNKS, 2, RC, BLK), jnp.bfloat16),
+                pltpu.SemaphoreType.DMA((CHUNKS,)),
+                pltpu.SemaphoreType.DMA((CHUNKS,)),
                 pltpu.VMEM((BLK, 2 * BLK), jnp.bfloat16),
                 pltpu.VMEM((BLK, 2 * BLK), jnp.bfloat16),
                 pltpu.SemaphoreType.DMA,

time: 38.1 us -> 35.3 us (0.927); the launches traced: 37.4 us -> 35.1 us
  Pallas kernels: 36.6 us -> 34.4 us
    pallas_call x1, Pallas kernels: 36.6 us -> 34.4 us  [step(): pl.pallas_call(functools.partial(kernel, count), out_shape=pltpu.VMEM(cur...]
where the time goes in v4:
time: 35.3 us; the launch traced here: 35.1 us
  Pallas kernels  34.4 us (97%)
  local copies, waits for them, and re-layouts  0.75 us (2%)
    pallas_call x1, Pallas kernels, step(): pl.pallas_call(functools.partial(kernel, count), out_shape=pltpu.VMEM(cur...  34.4 us
    unnamed x1, local copies, waits for them, and re-layouts  0.75 us

profile of v4, /device:TPU:1, one launch (start us, length us, event | category | flops | bytes accessed | tf_op | source)
XLA Modules:
  0.0 35.1 jit_solution(715142694854586928)
XLA Ops:
  0.0 34.4 %shard_map.46 = bf16[2,192,512]{2,1,0:T(8,128)(2,1)S(1)} custom-call(s32[1,4]{1,0:T(1,128)} %blk_ref.1, s32[1,4]{1,0:T(1,128)} %flg_ref.1, bf16[2,192,512]{2,1,0:T(8,128)(2,1)} %cur_hbm.1, bf16[1,2,1024,1024]{3,2,1,0:T(8,128)(2,1)} %inv_hbm.1), custom_call_target="tpu_custom_call" | custom-call | flops 1610612736 | bytes 4980736 | tf_op jit(solution)/shard_map/pallas_call | solution.py:356
  34.4 0.7 %copy.6 = bf16[2,192,512]{2,1,0:T(8,128)(2,1)} copy(bf16[2,192,512]{2,1,0:T(8,128)(2,1)S(1)} %shard_map.46) | data formatting | bytes 786432

commit v5 on v4

--- a/solution.py
+++ b/solution.py
@@ -42,8 +42,8 @@
 
 def kernel(
     count,
-    blk_ref,
-    flg_ref,
+    blk_hbm,
+    flg_hbm,
     cur_hbm,
     inv_hbm,
     out,
@@ -62,6 +62,8 @@
     back_send,
     back_recv,
     ready,
+    blk_ref,
+    flg_ref,
     relay,
     relay_send,
     relay_recv,
@@ -73,8 +75,6 @@
     me = lax.axis_index("groups")
     partner = partners(me, count)
 
-    load_cur = pltpu.make_async_copy(cur_hbm, cur, load_sem.at[0])
-    load_cur.start()
     barrier = pltpu.get_barrier_semaphore()
     first, last, hub = ends(me)
     before = lax.rem(me + count - 2 * COLS, count)
@@ -96,6 +96,14 @@
     def _():
         pl.semaphore_signal(barrier, inc=1, device_id=(before,), device_id_type=MESH)
 
+    load_cur = pltpu.make_async_copy(cur_hbm, cur, load_sem.at[0])
+    load_cur.start()
+    load_small = [
+        pltpu.make_async_copy(blk_hbm, blk_ref, load_sem.at[5]),
+        pltpu.make_async_copy(flg_hbm, flg_ref, load_sem.at[6]),
+    ]
+    for copy in load_small:
+        copy.start()
     load_mat = []
     for half in range(2):
         for part in range(2):
@@ -108,6 +116,8 @@
             )
             load_mat[-1].start()
 
+    for copy in load_small:
+        copy.wait()
     weight = [
         [
             jnp.where(blk_ref[0, r] == b, flg_ref[0, r], 0).astype(jnp.float32)
@@ -357,8 +367,8 @@
             functools.partial(kernel, count),
             out_shape=pltpu.VMEM(currents.shape, jnp.bfloat16),
             in_specs=[
-                pl.BlockSpec(memory_space=pltpu.SMEM),
-                pl.BlockSpec(memory_space=pltpu.SMEM),
+                pl.BlockSpec(memory_space=pl.ANY),
+                pl.BlockSpec(memory_space=pl.ANY),
                 pl.BlockSpec(memory_space=pl.ANY),
                 pl.BlockSpec(memory_space=pl.ANY),
             ],
@@ -373,12 +383,14 @@
                 pltpu.VMEM(pieces, jnp.bfloat16),
                 pltpu.VMEM(pieces, jnp.bfloat16),
                 pltpu.VMEM(pieces, jnp.bfloat16),
-                pltpu.SemaphoreType.DMA((5,)),
+                pltpu.SemaphoreType.DMA((7,)),
                 pltpu.SemaphoreType.DMA((CHUNKS, ROUNDS)),
                 pltpu.SemaphoreType.DMA((CHUNKS, ROUNDS)),
                 pltpu.SemaphoreType.DMA((CHUNKS, ROUNDS)),
                 pltpu.SemaphoreType.DMA((CHUNKS, ROUNDS)),
                 pltpu.SemaphoreType.REGULAR((ROUNDS,)),
+                pltpu.SMEM((1, ROUNDS), jnp.int32),
+                pltpu.SMEM((1, ROUNDS), jnp.int32),
                 pltpu.VMEM((CHUNKS, 2, RC, BLK), jnp.bfloat16),
                 pltpu.SemaphoreType.DMA((CHUNKS,)),
                 pltpu.SemaphoreType.DMA((CHUNKS,)),

time: 35.3 us -> 34.7 us (0.983)
  Pallas kernels: 34.4 us -> 33.8 us
    pallas_call x1, Pallas kernels: 34.4 us -> 33.8 us  [step(): pl.pallas_call(functools.partial(kernel, count), out_shape=pltpu.VMEM(cur...]
where the time goes in v5:
time: 34.7 us; the launch traced here: 34.6 us
  Pallas kernels  33.8 us (97%)
  local copies, waits for them, and re-layouts  0.75 us (2%)
    pallas_call x1, Pallas kernels, step(): pl.pallas_call(functools.partial(kernel, count), out_shape=pltpu.VMEM(cur...  33.8 us
    unnamed x1, local copies, waits for them, and re-layouts  0.75 us

profile of v5, /device:TPU:1, one launch (start us, length us, event | category | flops | bytes accessed | tf_op | source)
XLA Modules:
  0.0 34.6 jit_solution(12225660517928940820)
XLA Ops:
  0.0 33.8 %shard_map.46 = bf16[2,192,512]{2,1,0:T(8,128)(2,1)S(1)} custom-call(s32[1,4]{1,0:T(1,128)} %blk_hbm.1, s32[1,4]{1,0:T(1,128)} %flg_hbm.1, bf16[2,192,512]{2,1,0:T(8,128)(2,1)} %cur_hbm.1, bf16[1,2,1024,1024]{3,2,1,0:T(8,128)(2,1)} %inv_hbm.1), custom_call_target="tpu_custom_call" | custom-call | flops 1610612736 | bytes 4980736 | tf_op jit(solution)/shard_map/pallas_call | solution.py:366
  33.8 0.7 %copy.6 = bf16[2,192,512]{2,1,0:T(8,128)(2,1)} copy(bf16[2,192,512]{2,1,0:T(8,128)(2,1)S(1)} %shard_map.46) | data formatting | bytes 786432

commit v6 on v5

--- a/solution.py
+++ b/solution.py
@@ -302,10 +302,6 @@
                     pl.when(last[1] | jnp.logical_not(last[3]))(backs[c, r].start)
                 else:
                     unless(last[3], backs[c, r].start)
-        near = pl.ds(0, OWN)
-        local[c, :, :, near] += product(slot_rows, mat[near, pl.ds(ORDER, ORDER)]).reshape(
-            2, RC, OWN
-        )
 
     @pl.when(last[3])
     def _():
@@ -314,6 +310,12 @@
         for r in (2, 1, 0):
             for c in range(CHUNKS):
                 unless(last[1] if r == 1 else None, backs[c, r].start)
+
+    near = pl.ds(0, OWN)
+    for c in range(CHUNKS):
+        local[c, :, :, near] += product(
+            slot[c].reshape(2 * RC, ORDER), mat[near, pl.ds(ORDER, ORDER)]
+        ).reshape(2, RC, OWN)
 
     @pl.when(takes)
     def _():

time: 34.7 us -> 34.7 us (level)
  no operation moved by 1% of the time
where the time goes in v6:
time: 34.7 us; the launch traced here: 34.6 us
  Pallas kernels  33.8 us (97%)
  local copies, waits for them, and re-layouts  0.75 us (2%)
    pallas_call x1, Pallas kernels, step(): pl.pallas_call(functools.partial(kernel, count), out_shape=pltpu.VMEM(cur...  33.8 us
    unnamed x1, local copies, waits for them, and re-layouts  0.75 us

profile of v6, /device:TPU:1, one launch (start us, length us, event | category | flops | bytes accessed | tf_op | source)
XLA Modules:
  0.0 34.6 jit_solution(18179381988691310865)
XLA Ops:
  0.0 33.8 %shard_map.46 = bf16[2,192,512]{2,1,0:T(8,128)(2,1)S(1)} custom-call(s32[1,4]{1,0:T(1,128)} %blk_hbm.1, s32[1,4]{1,0:T(1,128)} %flg_hbm.1, bf16[2,192,512]{2,1,0:T(8,128)(2,1)} %cur_hbm.1, bf16[1,2,1024,1024]{3,2,1,0:T(8,128)(2,1)} %inv_hbm.1), custom_call_target="tpu_custom_call" | custom-call | flops 1610612736 | bytes 4980736 | tf_op jit(solution)/shard_map/pallas_call | solution.py:368
  33.8 0.7 %copy.6 = bf16[2,192,512]{2,1,0:T(8,128)(2,1)} copy(bf16[2,192,512]{2,1,0:T(8,128)(2,1)S(1)} %shard_map.46) | data formatting | bytes 786432

commit v7 on v5

--- a/solution.py
+++ b/solution.py
@@ -333,12 +333,17 @@
                 local[c, :, :, pl.ds(b * BLK, BLK)] += extra * weight[3][b]
 
     for c in range(CHUNKS):
-        for r in SEND_ORDER:
+        for r in (0, 1, 2):
             backs[c, r].wait_recv()
         for b in range(OWN // BLK):
             total = local[c, :, :, pl.ds(b * BLK, BLK)]
-            for r in range(ROUNDS):
+            for r in (0, 1, 2):
                 total += arrived[c, r].astype(jnp.float32) * weight[r][b]
+            local[c, :, :, pl.ds(b * BLK, BLK)] = total
+        backs[c, 3].wait_recv()
+        for b in range(OWN // BLK):
+            total = local[c, :, :, pl.ds(b * BLK, BLK)]
+            total += arrived[c, 3].astype(jnp.float32) * weight[3][b]
             out[:, pl.ds(c * RC, RC), pl.ds(b * BLK, BLK)] = total.astype(jnp.bfloat16)
     @pl.when(hub)
     def _():

time: 34.7 us -> 34.7 us (level)
  no operation moved by 1% of the time
where the time goes in v7:
time: 34.7 us; the launch traced here: 34.5 us
  Pallas kernels  33.8 us (97%)
  local copies, waits for them, and re-layouts  0.75 us (2%)
    pallas_call x1, Pallas kernels, step(): pl.pallas_call(functools.partial(kernel, count), out_shape=pltpu.VMEM(cur...  33.8 us
    unnamed x1, local copies, waits for them, and re-layouts  0.75 us

profile of v7, /device:TPU:1, one launch (start us, length us, event | category | flops | bytes accessed | tf_op | source)
XLA Modules:
  0.0 34.5 jit_solution(13931035889772342273)
XLA Ops:
  0.0 33.8 %shard_map.46 = bf16[2,192,512]{2,1,0:T(8,128)(2,1)S(1)} custom-call(s32[1,4]{1,0:T(1,128)} %blk_hbm.1, s32[1,4]{1,0:T(1,128)} %flg_hbm.1, bf16[2,192,512]{2,1,0:T(8,128)(2,1)} %cur_hbm.1, bf16[1,2,1024,1024]{3,2,1,0:T(8,128)(2,1)} %inv_hbm.1), custom_call_target="tpu_custom_call" | custom-call | flops 1610612736 | bytes 4980736 | tf_op jit(solution)/shard_map/pallas_call | solution.py:371
  33.8 0.7 %copy.6 = bf16[2,192,512]{2,1,0:T(8,128)(2,1)} copy(bf16[2,192,512]{2,1,0:T(8,128)(2,1)S(1)} %shard_map.46) | data formatting | bytes 786432
